TPU v7x, 256 devices: a whole 4x4x8 slice. The times are simulated.
256 devices in a mesh: blk: 16 (over z, y_lo), grp: 16 (over x, y_hi, core).
Axes of the slice: x: 4, y: 4 (y_hi: 2, y_lo: 2; y = y_hi * 2 + y_lo), z: 8, core: 2. Of those that a mesh axis runs over, the one named last changes fastest.
Arguments:
- state: float32 [2, 128, 32768], P(None, None, ('blk', 'grp')), may hold values from -3 to 3
- prev_slope: float32 [2, 128, 32768], P(None, None, ('blk', 'grp')), may hold values from -4 to 4
- positions: float32 [2, 32768], P(None, ('blk', 'grp')), may hold values from -1 to 1
- pump: float32 [32768], P(('blk', 'grp')), may hold values from -0.5 to 1.5
- detuning: float32 [32768], P(('blk', 'grp')), may hold values from -4 to 4
- kappa: float32 [6, 32768], P(None, ('blk', 'grp')), may hold values from 0.2 to 1
- neighbours: int32 [6, 32768], P(None, ('blk', 'grp')), may hold values from 0 to 255
- send_list: int32 [2, 16384], P(None, ('blk', 'grp')), may hold values from 0 to 127
Outputs:
- slope: float32 [2, 128, 32768], P(None, None, ('blk', 'grp'))
Inputs may be any that keep to these rules, and one draw needn't show every extreme that they name: `neighbours`: places below 128 are the block's own emitters, the next 64 those listed by the previous block, the last 64 those listed by the next block. `send_list`: places in the listing block.
All inputs are finite; a program needn't handle non-finite values.
Results may differ from a plain program's by a relative error of at most 0.0012.
Values may be sent and summed in bfloat16 or wider, within the bound.
A program may use at most 64 MiB of HBM per device.

v0:
```python
import math

import jax
import jax.numpy as jnp
from jax import lax
from jax.sharding import PartitionSpec as P

section_weight = 0.25
phase_rate = 60.0
alpha_factor = 2.0


def from_behind(array, axis, by):
    size = lax.axis_size(axis)
    return lax.ppermute(array, axis, [(i, (i + by) % size) for i in range(size)])


def with_halo(cells, sides, width):
    for axis, dim in sides:
        count = lax.axis_size(axis)
        ends = count - 1
        head = lax.slice_in_dim(cells, 0, width, axis=dim)
        tail = lax.slice_in_dim(cells, cells.shape[dim] - width, cells.shape[dim], axis=dim)
        cells = jnp.concatenate(
            [
                lax.ppermute(tail, axis, [(i, (i + 1) % count) for i in range(ends)]),
                cells,
                lax.ppermute(head, axis, [((i + 1) % count, i) for i in range(ends)]),
            ],
            axis=dim,
        )
    return cells


def kernel_table(source_place, target_place, scaled):
    horizontal = target_place[0][None, :] - source_place[0][:, None]
    vertical = target_place[1][None, :] - source_place[1][:, None]
    phase = phase_rate * (horizontal * horizontal + vertical * vertical)
    cosine = (scaled * jnp.cos(phase)).astype(jnp.bfloat16)
    sine_part = (scaled * jnp.sin(phase)).astype(jnp.bfloat16)
    return jnp.concatenate([cosine, sine_part], axis=1)


def block_columns(total, fields, source_place, target_place, scaled):
    members = fields.shape[1]
    targets = target_place.shape[1]
    kernel = kernel_table(source_place, target_place, scaled)
    flat = fields.reshape(2 * members, fields.shape[2])
    product = jnp.dot(flat, kernel, preferred_element_type=jnp.float32)
    real_part = product[:members, :targets] - product[members:, targets:]
    imag_part = product[:members, targets:] + product[members:, :targets]
    return total + jnp.stack([real_part, imag_part])


def local(state, prev_slope, positions, pump, detuning, kappa, neighbours, send_list):
    members = state.shape[1]
    rows_here = state.shape[2]
    block_count = lax.axis_size("blk")
    group_size = lax.axis_size("grp")
    scaled = 1.0 / math.sqrt(rows_here * block_count * group_size)
    section_field = state + section_weight * prev_slope
    section_half = section_field.astype(jnp.bfloat16)
    my_index = lax.axis_index("blk")
    target_place = lax.all_gather(positions, "grp", axis=1, tiled=True)
    source_place = lax.all_gather(positions, "blk", axis=1, tiled=True)
    targets = target_place.shape[1]

    def place_of(block_index):
        return lax.dynamic_slice_in_dim(
            source_place, block_index % block_count * rows_here, rows_here, 1
        )

    def add_block(total, fields, block_index):
        return block_columns(total, fields, place_of(block_index), target_place, scaled)

    empty = jnp.zeros((2, members, targets), jnp.float32)

    def advance(step, carry):
        total, carried = carry
        carried = from_behind(carried, "blk", 1)
        return (add_block(total, carried, my_index - step), carried)

    total = add_block(empty, section_half, my_index)
    total, carried = lax.fori_loop(1, block_count, advance, (total, section_half))
    fresnel = lax.psum_scatter(total, "grp", scatter_dimension=2, tiled=True)
    halo_width = send_list.shape[1]
    to_prev = jnp.take(section_field, send_list[1], axis=2)
    to_next = jnp.take(section_field, send_list[0], axis=2)
    padded = with_halo(
        jnp.concatenate([to_prev, to_next], axis=2), ((("blk", "grp"), 2),), halo_width
    )
    local_buffer = jnp.concatenate(
        [section_field, padded[:, :, :halo_width], padded[:, :, 3 * halo_width :]], axis=2
    )
    coupled = jnp.zeros((2, members, rows_here), jnp.float32)
    for neighbour_slot in range(kappa.shape[0]):
        picked = jnp.take(local_buffer, neighbours[neighbour_slot], axis=2)
        coupled = coupled + kappa[neighbour_slot] * picked
    real_field = section_field[0]
    imag_field = section_field[1]
    modulus = real_field * real_field + imag_field * imag_field
    linear_real = pump - modulus
    linear_imag = detuning - alpha_factor * modulus
    local_real = linear_real * real_field - linear_imag * imag_field
    local_imag = linear_real * imag_field + linear_imag * real_field
    slope_real = local_real + fresnel[0] - coupled[1]
    slope_imag = local_imag + fresnel[1] + coupled[0]
    return jnp.stack([slope_real, slope_imag])


def solution(mesh):
    placed = (
        P(None, None, ("blk", "grp")),
        P(None, None, ("blk", "grp")),
        P(None, ("blk", "grp")),
        P(("blk", "grp")),
        P(("blk", "grp")),
        P(None, ("blk", "grp")),
        P(None, ("blk", "grp")),
        P(None, ("blk", "grp")),
    )
    return jax.shard_map(
        local, mesh=mesh, in_specs=placed, out_specs=P(None, None, ("blk", "grp")), check_vma=False
    )
```

profile of v0, /device:TPU:8, one launch (start us, length us, event | category | flops | bytes accessed | tf_op | source)
XLA Modules:
  0.0 356.1 jit_solution(1901654275807691150)
XLA Ops:
  6.5 33.4 %all_gather.7 = f32[2,2048]{1,0:T(2,128)S(1)} all-gather(f32[2,128]{1,0:T(2,128)} %param.16), channel_id=1, replica_groups=mesh['blk'=16,'grp'=16] {'blk'}, dimensions={1}, use_global_device_ids=true | all-gather | bytes 17408 | tf_op jit(solution)/shard_map/all_gather | solution.py:65
  39.9 23.9 %all_gather.6 = f32[2,2048]{1,0:T(2,128)S(1)} all-gather(f32[2,128]{1,0:T(2,128)} %param.16), channel_id=1, replica_groups=mesh['blk'=16,'grp'=16] {'grp'}, dimensions={1}, use_global_device_ids=true | all-gather | bytes 17408 | tf_op jit(solution)/shard_map/all_gather | solution.py:64
  64.9 4.3 %multiply_convert_fusion.3 = (bf16[128,2048]{1,0:T(8,128)(2,1)S(1)}, bf16[128,2048]{1,0:T(8,128)(2,1)S(1)}) fusion(f32[128]{0:T(128)S(1)} %get-tuple-element.252, f32[2048]{0:T(1024)S(1)} %bitcast.118, f32[128]{0:T(128)S(1)} %get-tuple-element.251, f32[2048]{0:T(1024)S(1)} %bitcast.117), kind=kLoop, calls=%fused_computation.34 | loop fusion | flops 2621440 | bytes 1065984 | tf_op jit(solution)/shard_map/convert_element_type | solution.py:39
  73.6 119.0 %while.17 = (s32[]{:T(128)}, f32[2,128,2048]{1,2,0:T(8,128)S(1)}, bf16[2,128,128]{2,1,0:T(8,128)(2,1)S(1)}, f32[2,2048]{1,0:T(2,128)S(1)}, s32[]{:T(128)}, /*ind...) while((s32[]{:T(128)}, f32[2,128,2048]{1,2,0:T(8,128)S(1)}, ...), condition=%wide.region_1.2_spmd, body=%wide.region_0.1_spmd.sunk | while | flops 274726944 | bytes 19387720 | solution.py:84
  73.6 2.9 collective-permute-start
  76.5 4.3 %multiply_convert_fusion.5 = (bf16[128,2048]{1,0:T(8,128)(2,1)S(1)}, bf16[128,2048]{1,0:T(8,128)(2,1)S(1)}) fusion(f32[128]{0:T(128)S(1)} %get-tuple-element.306, f32[2048]{0:T(1024)S(1)} %bitcast.115, f32[128]{0:T(128)S(1)} %get-tuple-element.308, f32[2048]{0:T(1024)S(1)} %bitcast.114), kind=kLoop, calls=%fused_computation.18.clone.1 | loop fusion | flops 2621440 | bytes 1065984 | tf_op jit(solution)/shard_map/while/body/eval_jaxpr/convert_element_type | solution.py:39
  83.3 4.3 %multiply_convert_fusion.5 = (bf16[128,2048]{1,0:T(8,128)(2,1)S(1)}, bf16[128,2048]{1,0:T(8,128)(2,1)S(1)}) fusion(f32[128]{0:T(128)S(1)} %get-tuple-element.306, f32[2048]{0:T(1024)S(1)} %bitcast.115, f32[128]{0:T(128)S(1)} %get-tuple-element.308, f32[2048]{0:T(1024)S(1)} %bitcast.114), kind=kLoop, calls=%fused_computation.18.clone.1 | loop fusion | flops 2621440 | bytes 1065984 | tf_op jit(solution)/shard_map/while/body/eval_jaxpr/convert_element_type | solution.py:39
  90.0 4.3 %multiply_convert_fusion.5 = (bf16[128,2048]{1,0:T(8,128)(2,1)S(1)}, bf16[128,2048]{1,0:T(8,128)(2,1)S(1)}) fusion(f32[128]{0:T(128)S(1)} %get-tuple-element.306, f32[2048]{0:T(1024)S(1)} %bitcast.115, f32[128]{0:T(128)S(1)} %get-tuple-element.308, f32[2048]{0:T(1024)S(1)} %bitcast.114), kind=kLoop, calls=%fused_computation.18.clone.1 | loop fusion | flops 2621440 | bytes 1065984 | tf_op jit(solution)/shard_map/while/body/eval_jaxpr/convert_element_type | solution.py:39
  97.4 4.3 %multiply_convert_fusion.5 = (bf16[128,2048]{1,0:T(8,128)(2,1)S(1)}, bf16[128,2048]{1,0:T(8,128)(2,1)S(1)}) fusion(f32[128]{0:T(128)S(1)} %get-tuple-element.306, f32[2048]{0:T(1024)S(1)} %bitcast.115, f32[128]{0:T(128)S(1)} %get-tuple-element.308, f32[2048]{0:T(1024)S(1)} %bitcast.114), kind=kLoop, calls=%fused_computation.18.clone.1 | loop fusion | flops 2621440 | bytes 1065984 | tf_op jit(solution)/shard_map/while/body/eval_jaxpr/convert_element_type | solution.py:39
  105.3 4.3 %multiply_convert_fusion.5 = (bf16[128,2048]{1,0:T(8,128)(2,1)S(1)}, bf16[128,2048]{1,0:T(8,128)(2,1)S(1)}) fusion(f32[128]{0:T(128)S(1)} %get-tuple-element.306, f32[2048]{0:T(1024)S(1)} %bitcast.115, f32[128]{0:T(128)S(1)} %get-tuple-element.308, f32[2048]{0:T(1024)S(1)} %bitcast.114), kind=kLoop, calls=%fused_computation.18.clone.1 | loop fusion | flops 2621440 | bytes 1065984 | tf_op jit(solution)/shard_map/while/body/eval_jaxpr/convert_element_type | solution.py:39
  113.2 4.3 %multiply_convert_fusion.5 = (bf16[128,2048]{1,0:T(8,128)(2,1)S(1)}, bf16[128,2048]{1,0:T(8,128)(2,1)S(1)}) fusion(f32[128]{0:T(128)S(1)} %get-tuple-element.306, f32[2048]{0:T(1024)S(1)} %bitcast.115, f32[128]{0:T(128)S(1)} %get-tuple-element.308, f32[2048]{0:T(1024)S(1)} %bitcast.114), kind=kLoop, calls=%fused_computation.18.clone.1 | loop fusion | flops 2621440 | bytes 1065984 | tf_op jit(solution)/shard_map/while/body/eval_jaxpr/convert_element_type | solution.py:39
  121.1 4.3 %multiply_convert_fusion.5 = (bf16[128,2048]{1,0:T(8,128)(2,1)S(1)}, bf16[128,2048]{1,0:T(8,128)(2,1)S(1)}) fusion(f32[128]{0:T(128)S(1)} %get-tuple-element.306, f32[2048]{0:T(1024)S(1)} %bitcast.115, f32[128]{0:T(128)S(1)} %get-tuple-element.308, f32[2048]{0:T(1024)S(1)} %bitcast.114), kind=kLoop, calls=%fused_computation.18.clone.1 | loop fusion | flops 2621440 | bytes 1065984 | tf_op jit(solution)/shard_map/while/body/eval_jaxpr/convert_element_type | solution.py:39
  125.4 2.5 collective-permute-done
  129.5 4.3 %multiply_convert_fusion.5 = (bf16[128,2048]{1,0:T(8,128)(2,1)S(1)}, bf16[128,2048]{1,0:T(8,128)(2,1)S(1)}) fusion(f32[128]{0:T(128)S(1)} %get-tuple-element.306, f32[2048]{0:T(1024)S(1)} %bitcast.115, f32[128]{0:T(128)S(1)} %get-tuple-element.308, f32[2048]{0:T(1024)S(1)} %bitcast.114), kind=kLoop, calls=%fused_computation.18.clone.1 | loop fusion | flops 2621440 | bytes 1065984 | tf_op jit(solution)/shard_map/while/body/eval_jaxpr/convert_element_type | solution.py:39
  137.2 4.3 %multiply_convert_fusion.5 = (bf16[128,2048]{1,0:T(8,128)(2,1)S(1)}, bf16[128,2048]{1,0:T(8,128)(2,1)S(1)}) fusion(f32[128]{0:T(128)S(1)} %get-tuple-element.306, f32[2048]{0:T(1024)S(1)} %bitcast.115, f32[128]{0:T(128)S(1)} %get-tuple-element.308, f32[2048]{0:T(1024)S(1)} %bitcast.114), kind=kLoop, calls=%fused_computation.18.clone.1 | loop fusion | flops 2621440 | bytes 1065984 | tf_op jit(solution)/shard_map/while/body/eval_jaxpr/convert_element_type | solution.py:39
  145.0 4.3 %multiply_convert_fusion.5 = (bf16[128,2048]{1,0:T(8,128)(2,1)S(1)}, bf16[128,2048]{1,0:T(8,128)(2,1)S(1)}) fusion(f32[128]{0:T(128)S(1)} %get-tuple-element.306, f32[2048]{0:T(1024)S(1)} %bitcast.115, f32[128]{0:T(128)S(1)} %get-tuple-element.308, f32[2048]{0:T(1024)S(1)} %bitcast.114), kind=kLoop, calls=%fused_computation.18.clone.1 | loop fusion | flops 2621440 | bytes 1065984 | tf_op jit(solution)/shard_map/while/body/eval_jaxpr/convert_element_type | solution.py:39
  152.9 4.3 %multiply_convert_fusion.5 = (bf16[128,2048]{1,0:T(8,128)(2,1)S(1)}, bf16[128,2048]{1,0:T(8,128)(2,1)S(1)}) fusion(f32[128]{0:T(128)S(1)} %get-tuple-element.306, f32[2048]{0:T(1024)S(1)} %bitcast.115, f32[128]{0:T(128)S(1)} %get-tuple-element.308, f32[2048]{0:T(1024)S(1)} %bitcast.114), kind=kLoop, calls=%fused_computation.18.clone.1 | loop fusion | flops 2621440 | bytes 1065984 | tf_op jit(solution)/shard_map/while/body/eval_jaxpr/convert_element_type | solution.py:39
  160.8 4.3 %multiply_convert_fusion.5 = (bf16[128,2048]{1,0:T(8,128)(2,1)S(1)}, bf16[128,2048]{1,0:T(8,128)(2,1)S(1)}) fusion(f32[128]{0:T(128)S(1)} %get-tuple-element.306, f32[2048]{0:T(1024)S(1)} %bitcast.115, f32[128]{0:T(128)S(1)} %get-tuple-element.308, f32[2048]{0:T(1024)S(1)} %bitcast.114), kind=kLoop, calls=%fused_computation.18.clone.1 | loop fusion | flops 2621440 | bytes 1065984 | tf_op jit(solution)/shard_map/while/body/eval_jaxpr/convert_element_type | solution.py:39
  168.7 4.3 %multiply_convert_fusion.5 = (bf16[128,2048]{1,0:T(8,128)(2,1)S(1)}, bf16[128,2048]{1,0:T(8,128)(2,1)S(1)}) fusion(f32[128]{0:T(128)S(1)} %get-tuple-element.306, f32[2048]{0:T(1024)S(1)} %bitcast.115, f32[128]{0:T(128)S(1)} %get-tuple-element.308, f32[2048]{0:T(1024)S(1)} %bitcast.114), kind=kLoop, calls=%fused_computation.18.clone.1 | loop fusion | flops 2621440 | bytes 1065984 | tf_op jit(solution)/shard_map/while/body/eval_jaxpr/convert_element_type | solution.py:39
  177.0 4.3 %multiply_convert_fusion.5 = (bf16[128,2048]{1,0:T(8,128)(2,1)S(1)}, bf16[128,2048]{1,0:T(8,128)(2,1)S(1)}) fusion(f32[128]{0:T(128)S(1)} %get-tuple-element.306, f32[2048]{0:T(1024)S(1)} %bitcast.115, f32[128]{0:T(128)S(1)} %get-tuple-element.308, f32[2048]{0:T(1024)S(1)} %bitcast.114), kind=kLoop, calls=%fused_computation.18.clone.1 | loop fusion | flops 2621440 | bytes 1065984 | tf_op jit(solution)/shard_map/while/body/eval_jaxpr/convert_element_type | solution.py:39
  184.9 4.3 %multiply_convert_fusion.5 = (bf16[128,2048]{1,0:T(8,128)(2,1)S(1)}, bf16[128,2048]{1,0:T(8,128)(2,1)S(1)}) fusion(f32[128]{0:T(128)S(1)} %get-tuple-element.306, f32[2048]{0:T(1024)S(1)} %bitcast.115, f32[128]{0:T(128)S(1)} %get-tuple-element.308, f32[2048]{0:T(1024)S(1)} %bitcast.114), kind=kLoop, calls=%fused_computation.18.clone.1 | loop fusion | flops 2621440 | bytes 1065984 | tf_op jit(solution)/shard_map/while/body/eval_jaxpr/convert_element_type | solution.py:39
  192.6 8.5 %copy.24 = f32[2,128,2048]{1,0,2:T(2,128)} copy(f32[2,128,2048]{1,2,0:T(8,128)S(1)} %get-tuple-element.162) | data formatting | bytes 4194304 | tf_op jit(solution)/shard_map/while | solution.py:84
  205.4 5.8 %collective-permute-start.2 = (f32[2,128,64]{2,1,0:T(8,128)S(1)}, f32[2,128,64]{2,1,0:T(8,128)S(1)}, u32[]{:S(2)}, u32[]{:S(2)}) collective-permute-start(f32[2,128,64]{2,1,0:T(8,128)S(1)} %select_bitcast_fusion), channel_id=1, source_target_pairs={{1,0},{2,1},{3,2},{4,3},{5,4},{6,5},{7,6},{8,7},{9,8},{10,9},{11,1... | collective-permute-start | bytes 196616 | tf_op jit(solution)/shard_map/ppermute | solution.py:28
  219.1 128.1 %all-reduce.3.cloned.1.call-done = f32[2,128,2048]{1,0,2:T(2,128)} async-done(((f32[2,128,2048]{1,0,2:T(2,128)}), f32[2,128,2048]{1,0,2:T(2,128)}) %all-reduce.3.cloned.1.call-update) | async-done | bytes 2097168
  (194 shorter events, 66.7 us)
Async XLA Ops:
  6.5 340.7 %all-reduce.3.cloned.1.call-start = ((), (), s32[]{:S(2)}) async-start(), calls=%async_computation | async-start | bytes 4194304
  73.6 7.2 %collective-permute-start = (bf16[2,128,128]{2,1,0:T(8,128)(2,1)S(1)}, bf16[2,128,128]{2,1,0:T(8,128)(2,1)S(1)}, u32[]{:S(2)}, u32[]{:S(2)}) collective-permute-start(bf16[2,128,128]{2,1,0:T(8,128)(2,1)S(1)} %get-tuple-element.328), channel_id=1, source_target_pairs={{0,16},{16,32},{32,48},{48,64},{64,80},{80,96},{96,112},{112,128},... | collective-permute-start | bytes 196616 | tf_op jit(solution)/shard_map/while/body/eval_jaxpr/ppermute | solution.py:15
  82.3 5.6 %collective-permute-start = (bf16[2,128,128]{2,1,0:T(8,128)(2,1)S(1)}, bf16[2,128,128]{2,1,0:T(8,128)(2,1)S(1)}, u32[]{:S(2)}, u32[]{:S(2)}) collective-permute-start(bf16[2,128,128]{2,1,0:T(8,128)(2,1)S(1)} %get-tuple-element.328), channel_id=1, source_target_pairs={{0,16},{16,32},{32,48},{48,64},{64,80},{80,96},{96,112},{112,128},... | collective-permute-start | bytes 196616 | tf_op jit(solution)/shard_map/while/body/eval_jaxpr/ppermute | solution.py:15
  89.4 6.5 %collective-permute-start = (bf16[2,128,128]{2,1,0:T(8,128)(2,1)S(1)}, bf16[2,128,128]{2,1,0:T(8,128)(2,1)S(1)}, u32[]{:S(2)}, u32[]{:S(2)}) collective-permute-start(bf16[2,128,128]{2,1,0:T(8,128)(2,1)S(1)} %get-tuple-element.328), channel_id=1, source_target_pairs={{0,16},{16,32},{32,48},{48,64},{64,80},{80,96},{96,112},{112,128},... | collective-permute-start | bytes 196616 | tf_op jit(solution)/shard_map/while/body/eval_jaxpr/ppermute | solution.py:15
  97.2 6.5 %collective-permute-start = (bf16[2,128,128]{2,1,0:T(8,128)(2,1)S(1)}, bf16[2,128,128]{2,1,0:T(8,128)(2,1)S(1)}, u32[]{:S(2)}, u32[]{:S(2)}) collective-permute-start(bf16[2,128,128]{2,1,0:T(8,128)(2,1)S(1)} %get-tuple-element.328), channel_id=1, source_target_pairs={{0,16},{16,32},{32,48},{48,64},{64,80},{80,96},{96,112},{112,128},... | collective-permute-start | bytes 196616 | tf_op jit(solution)/shard_map/while/body/eval_jaxpr/ppermute | solution.py:15
  105.1 6.5 %collective-permute-start = (bf16[2,128,128]{2,1,0:T(8,128)(2,1)S(1)}, bf16[2,128,128]{2,1,0:T(8,128)(2,1)S(1)}, u32[]{:S(2)}, u32[]{:S(2)}) collective-permute-start(bf16[2,128,128]{2,1,0:T(8,128)(2,1)S(1)} %get-tuple-element.328), channel_id=1, source_target_pairs={{0,16},{16,32},{32,48},{48,64},{64,80},{80,96},{96,112},{112,128},... | collective-permute-start | bytes 196616 | tf_op jit(solution)/shard_map/while/body/eval_jaxpr/ppermute | solution.py:15
  113.0 6.5 %collective-permute-start = (bf16[2,128,128]{2,1,0:T(8,128)(2,1)S(1)}, bf16[2,128,128]{2,1,0:T(8,128)(2,1)S(1)}, u32[]{:S(2)}, u32[]{:S(2)}) collective-permute-start(bf16[2,128,128]{2,1,0:T(8,128)(2,1)S(1)} %get-tuple-element.328), channel_id=1, source_target_pairs={{0,16},{16,32},{32,48},{48,64},{64,80},{80,96},{96,112},{112,128},... | collective-permute-start | bytes 196616 | tf_op jit(solution)/shard_map/while/body/eval_jaxpr/ppermute | solution.py:15
  120.9 7.0 %collective-permute-start = (bf16[2,128,128]{2,1,0:T(8,128)(2,1)S(1)}, bf16[2,128,128]{2,1,0:T(8,128)(2,1)S(1)}, u32[]{:S(2)}, u32[]{:S(2)}) collective-permute-start(bf16[2,128,128]{2,1,0:T(8,128)(2,1)S(1)} %get-tuple-element.328), channel_id=1, source_target_pairs={{0,16},{16,32},{32,48},{48,64},{64,80},{80,96},{96,112},{112,128},... | collective-permute-start | bytes 196616 | tf_op jit(solution)/shard_map/while/body/eval_jaxpr/ppermute | solution.py:15
  129.3 6.2 %collective-permute-start = (bf16[2,128,128]{2,1,0:T(8,128)(2,1)S(1)}, bf16[2,128,128]{2,1,0:T(8,128)(2,1)S(1)}, u32[]{:S(2)}, u32[]{:S(2)}) collective-permute-start(bf16[2,128,128]{2,1,0:T(8,128)(2,1)S(1)} %get-tuple-element.328), channel_id=1, source_target_pairs={{0,16},{16,32},{32,48},{48,64},{64,80},{80,96},{96,112},{112,128},... | collective-permute-start | bytes 196616 | tf_op jit(solution)/shard_map/while/body/eval_jaxpr/ppermute | solution.py:15
  137.0 6.4 %collective-permute-start = (bf16[2,128,128]{2,1,0:T(8,128)(2,1)S(1)}, bf16[2,128,128]{2,1,0:T(8,128)(2,1)S(1)}, u32[]{:S(2)}, u32[]{:S(2)}) collective-permute-start(bf16[2,128,128]{2,1,0:T(8,128)(2,1)S(1)} %get-tuple-element.328), channel_id=1, source_target_pairs={{0,16},{16,32},{32,48},{48,64},{64,80},{80,96},{96,112},{112,128},... | collective-permute-start | bytes 196616 | tf_op jit(solution)/shard_map/while/body/eval_jaxpr/ppermute | solution.py:15
  144.9 6.5 %collective-permute-start = (bf16[2,128,128]{2,1,0:T(8,128)(2,1)S(1)}, bf16[2,128,128]{2,1,0:T(8,128)(2,1)S(1)}, u32[]{:S(2)}, u32[]{:S(2)}) collective-permute-start(bf16[2,128,128]{2,1,0:T(8,128)(2,1)S(1)} %get-tuple-element.328), channel_id=1, source_target_pairs={{0,16},{16,32},{32,48},{48,64},{64,80},{80,96},{96,112},{112,128},... | collective-permute-start | bytes 196616 | tf_op jit(solution)/shard_map/while/body/eval_jaxpr/ppermute | solution.py:15
  152.8 6.5 %collective-permute-start = (bf16[2,128,128]{2,1,0:T(8,128)(2,1)S(1)}, bf16[2,128,128]{2,1,0:T(8,128)(2,1)S(1)}, u32[]{:S(2)}, u32[]{:S(2)}) collective-permute-start(bf16[2,128,128]{2,1,0:T(8,128)(2,1)S(1)} %get-tuple-element.328), channel_id=1, source_target_pairs={{0,16},{16,32},{32,48},{48,64},{64,80},{80,96},{96,112},{112,128},... | collective-permute-start | bytes 196616 | tf_op jit(solution)/shard_map/while/body/eval_jaxpr/ppermute | solution.py:15
  160.7 6.5 %collective-permute-start = (bf16[2,128,128]{2,1,0:T(8,128)(2,1)S(1)}, bf16[2,128,128]{2,1,0:T(8,128)(2,1)S(1)}, u32[]{:S(2)}, u32[]{:S(2)}) collective-permute-start(bf16[2,128,128]{2,1,0:T(8,128)(2,1)S(1)} %get-tuple-element.328), channel_id=1, source_target_pairs={{0,16},{16,32},{32,48},{48,64},{64,80},{80,96},{96,112},{112,128},... | collective-permute-start | bytes 196616 | tf_op jit(solution)/shard_map/while/body/eval_jaxpr/ppermute | solution.py:15
  168.6 6.8 %collective-permute-start = (bf16[2,128,128]{2,1,0:T(8,128)(2,1)S(1)}, bf16[2,128,128]{2,1,0:T(8,128)(2,1)S(1)}, u32[]{:S(2)}, u32[]{:S(2)}) collective-permute-start(bf16[2,128,128]{2,1,0:T(8,128)(2,1)S(1)} %get-tuple-element.328), channel_id=1, source_target_pairs={{0,16},{16,32},{32,48},{48,64},{64,80},{80,96},{96,112},{112,128},... | collective-permute-start | bytes 196616 | tf_op jit(solution)/shard_map/while/body/eval_jaxpr/ppermute | solution.py:15
  176.8 6.5 %collective-permute-start = (bf16[2,128,128]{2,1,0:T(8,128)(2,1)S(1)}, bf16[2,128,128]{2,1,0:T(8,128)(2,1)S(1)}, u32[]{:S(2)}, u32[]{:S(2)}) collective-permute-start(bf16[2,128,128]{2,1,0:T(8,128)(2,1)S(1)} %get-tuple-element.328), channel_id=1, source_target_pairs={{0,16},{16,32},{32,48},{48,64},{64,80},{80,96},{96,112},{112,128},... | collective-permute-start | bytes 196616 | tf_op jit(solution)/shard_map/while/body/eval_jaxpr/ppermute | solution.py:15
  184.7 6.5 %collective-permute-start = (bf16[2,128,128]{2,1,0:T(8,128)(2,1)S(1)}, bf16[2,128,128]{2,1,0:T(8,128)(2,1)S(1)}, u32[]{:S(2)}, u32[]{:S(2)}) collective-permute-start(bf16[2,128,128]{2,1,0:T(8,128)(2,1)S(1)} %get-tuple-element.328), channel_id=1, source_target_pairs={{0,16},{16,32},{32,48},{48,64},{64,80},{80,96},{96,112},{112,128},... | collective-permute-start | bytes 196616 | tf_op jit(solution)/shard_map/while/body/eval_jaxpr/ppermute | solution.py:15
  201.2 0.7 copy-start.2
  201.2 10.0 %copy-start.5 = (u32[256]{0:T(256)S(1)}, u32[256]{0:T(256)}, u32[]{:S(2)}) copy-start(u32[256]{0:T(256)} %constant.141) | copy-start | bytes 3076
  201.2 11.2 %copy-start.1 = (s32[6,128]{1,0:T(8,128)S(1)}, s32[6,128]{1,0:T(8,128)}, u32[]{:S(2)}) copy-start(s32[6,128]{1,0:T(8,128)} %param.20) | copy-start | bytes 9220
  201.2 11.3 %copy-start = (f32[6,128]{1,0:T(8,128)S(1)}, f32[6,128]{1,0:T(8,128)}, u32[]{:S(2)}) copy-start(f32[6,128]{1,0:T(8,128)} %param.19) | copy-start | bytes 9220
  202.7 9.8 %collective-permute-start.1 = (f32[2,128,64]{2,1,0:T(8,128)S(1)}, f32[2,128,64]{2,1,0:T(8,128)S(1)}, u32[]{:S(2)}, u32[]{:S(2)}) collective-permute-start(f32[2,128,64]{2,1,0:T(8,128)S(1)} %select_bitcast_fusion.1), channel_id=1, source_target_pairs={{0,1},{1,2},{2,3},{3,4},{4,5},{5,6},{6,7},{7,8},{8,9},{9,10},{10,1... | collective-permute-start | bytes 196616 | tf_op jit(solution)/shard_map/ppermute | solution.py:26
  205.4 8.3 %collective-permute-start.2 = (f32[2,128,64]{2,1,0:T(8,128)S(1)}, f32[2,128,64]{2,1,0:T(8,128)S(1)}, u32[]{:S(2)}, u32[]{:S(2)}) collective-permute-start(f32[2,128,64]{2,1,0:T(8,128)S(1)} %select_bitcast_fusion), channel_id=1, source_target_pairs={{1,0},{2,1},{3,2},{4,3},{5,4},{6,5},{7,6},{8,7},{9,8},{10,9},{11,1... | collective-permute-start | bytes 196616 | tf_op jit(solution)/shard_map/ppermute | solution.py:28
  214.7 133.7 %copy-start.3 = (f32[128]{0:T(128)S(1)}, f32[128]{0:T(128)}, u32[]{:S(2)}) copy-start(f32[128]{0:T(128)} %param.18) | copy-start | bytes 1540
  214.8 133.7 %copy-start.4 = (f32[128]{0:T(128)S(1)}, f32[128]{0:T(128)}, u32[]{:S(2)}) copy-start(f32[128]{0:T(128)} %param.17) | copy-start | bytes 1540
Sparse Core Ops, SparseCore 0:
  201.3 145.8 all-reduce.2
where the time goes:
time: 357 us; the launch traced here: 356 us
  waiting for transfers between devices  156 us (44%)
  other arithmetic  82.2 us (23%)
  blocking collectives  57.3 us (16%)
  local copies, waits for them, and re-layouts  20.2 us (6%)
  between operations  14.4 us (4%)
  starting transfers between devices  13.1 us (4%)
  matrix products  11.8 us (3%)
    unnamed x2, waiting for transfers between devices  128 us
    convert_element_type x16, other arithmetic, kernel_table(): cosine = (scaled * jnp.cos(phase)).astype(jnp.bfloat16)  68.5 us
    all_gather x1, blocking collectives, local(): source_place = lax.all_gather(positions, 'blk', axis=1, tiled=True)  33.4 us
    ppermute x15, waiting for transfers between devices, from_behind(): lax.ppermute(array, axis, [(i, (i + by) % size) for i in range(size)])  26.5 us
    all_gather x1, blocking collectives, local(): target_place = lax.all_gather(positions, 'grp', axis=1, tiled=True)  23.9 us
    dot_general x16, matrix products, block_columns(): product = jnp.dot(flat, kernel, preferred_element_type=jnp.float32)  11.8 us
    while x2, local copies, waits for them, and re-layouts, local(): lax.fori_loop(1, block_count, advance, (total, section_half))  10.4 us
  transfers between devices with their start and end apart: 18, of which 16 were waited for; matrix products, arithmetic and copies ran while one was open for 20% of the time, Pallas kernels for 0%

commit v1 on v0

v1 whole, which is shorter than its diff:
```python
import math

import jax
import jax.numpy as jnp
from jax import lax
from jax.experimental import pallas as pl
from jax.experimental.pallas import tpu as pltpu
from jax.sharding import PartitionSpec as P

section_weight = 0.25
phase_rate = 60.0
alpha_factor = 2.0

MESH = pl.DeviceIdType.MESH
ROOT_HALF = 2.0**-0.5
MAGIC = 12582912.0
SINE = tuple(2.0**0.25 * c for c in (3.14158202, -5.1671428, 2.54189902, -0.55463618))


def place():
    band, member = lax.axis_index("blk"), lax.axis_index("grp")
    return band // 2, (member // 2) % 2 * 2 + band % 2, member // 4, member % 2


def device(z, y, x, core):
    return (z * 2 + y % 2, x * 4 + y // 2 * 2 + core)


def column_peer(k):
    z, y, x, core = place()
    return device((z + k // 2) % 8, y, x, (core + k) % 2)


def plane_peer(k, sign=1):
    z, y, x, core = place()
    return device(z, (y + sign * (k % 4)) % 4, (x + sign * (k // 4)) % 4, core)


def listed_peer(step):
    index = (lax.axis_index("blk") * 16 + lax.axis_index("grp") + step) % 256
    return (index // 16, index % 16)


def wave(turns):
    f = turns - jnp.round(turns)
    z = f * f
    p = SINE[3] * z + SINE[2]
    p = p * z + SINE[1]
    p = p * z + SINE[0]
    u = f * p
    w = u * u
    a = 2.0 * ROOT_HALF - w
    return ROOT_HALF - w, (u * a) * lax.rsqrt(a)


def exact_dot(a, b):
    return jnp.dot(a, b, precision=lax.Precision.HIGHEST, preferred_element_type=jnp.float32)


def kernel(
    state, prev_slope, positions, pump, detuning, kappa, neighbours, send_list, out,
    fields, source_at, target_at, table, partial, arrived, own_sum, listed, halo,
    f_send, f_recv, s_send, s_recv, t_send, t_recv, p_send, p_recv, h_send, h_recv,
):
    n = 128
    barrier = pltpu.get_barrier_semaphore()
    for k in range(1, 16):
        pl.semaphore_signal(barrier, inc=1, device_id=column_peer(k), device_id_type=MESH)
        pl.semaphore_signal(barrier, inc=1, device_id=plane_peer(k), device_id_type=MESH)
    for step in (1, 255):
        pl.semaphore_signal(barrier, inc=1, device_id=listed_peer(step), device_id_type=MESH)

    field = [state[i] + section_weight * prev_slope[i] for i in range(2)]
    field_t = jnp.concatenate([field[0].T, field[1].T], axis=1)
    fields[pl.ds(0, n), :] = field_t.astype(jnp.bfloat16)
    scaled = positions[...] * math.sqrt(phase_rate / (2.0 * math.pi))
    source_at[0] = scaled
    target_at[0] = scaled
    lists = jnp.concatenate([send_list[0:1, :], send_list[1:2, :]], axis=1)
    rows = lax.broadcasted_iota(jnp.int32, (n, n), 0)
    chosen = jnp.where(rows == lists, 1.0, 0.0)
    listed[...] = exact_dot(chosen.T, field_t)

    pl.semaphore_wait(barrier, 32)

    pending = []

    def send(src, dst, send_sem, recv_sem, peer):
        copy = pltpu.make_async_remote_copy(
            src_ref=src, dst_ref=dst, send_sem=send_sem, recv_sem=recv_sem, device_id=peer, device_id_type=MESH
        )
        copy.start()
        pending.append(copy)
        return copy

    def block(k):
        return fields.at[pl.ds(k * n, n)]

    s_copies, t_copies = {}, {}
    for k in range(1, 16):
        s_copies[k] = send(source_at.at[0], source_at.at[k], s_send.at[k], s_recv.at[k], column_peer(k))
        t_copies[k] = send(target_at.at[0], target_at.at[k], t_send.at[k], t_recv.at[k], plane_peer(k, -1))
    f_copies = {1: send(block(0), block(1), f_send.at[1], f_recv.at[1], column_peer(1))}
    for step in (1, 7, 2, 6, 3, 5, 4):
        k = 2 * step
        f_copies[k] = send(block(0), block(k), f_send.at[k], f_recv.at[k], column_peer(k))
    h_copies = [
        send(listed.at[pl.ds(i * 64, 64)], halo.at[pl.ds(i * 64, 64)], h_send.at[i], h_recv.at[i], listed_peer(step))
        for i, step in enumerate((1, 255))
    ]

    for k in range(1, 16):
        s_copies[k].wait_recv()
        t_copies[k].wait_recv()

    def tabulate(i, _):
        t, s = i // 4, i % 4 * 4
        tx = jnp.broadcast_to(target_at[t, 0:1, :], (n, n)).T
        ty = jnp.broadcast_to(target_at[t, 1:2, :], (n, n)).T
        for j in range(4):
            dx = tx - source_at[s + j, 0:1, :]
            dy = ty - source_at[s + j, 1:2, :]
            cosine, sine = wave(dx * dx + dy * dy)
            at = pl.multiple_of((s + j) * n, n)
            table[t, :, pl.ds(at, n)] = cosine.astype(jnp.bfloat16)
            table[t, :, pl.ds(16 * n + at, n)] = sine.astype(jnp.bfloat16)
        return 0

    lax.fori_loop(0, 64, tabulate, 0)

    for step in (1, 7, 2, 6, 3, 5, 4):
        k = 2 * step
        f_copies[k].wait_recv()
        f_copies[k + 1] = send(block(k), block(k + 1), f_send.at[k + 1], f_recv.at[k + 1], column_peer(1))
    for step in range(8):
        f_copies[2 * step + 1].wait_recv()

    def turned(k, _):
        here = fields[pl.ds(pl.multiple_of(k * n, n), n), :]
        fields[pl.ds(pl.multiple_of((k + 16) * n, n), n), :] = jnp.concatenate([-here[:, n:], here[:, :n]], axis=1)
        return 0

    lax.fori_loop(0, 16, turned, 0)

    def total(t):
        return jnp.dot(table[t], fields[...], preferred_element_type=jnp.float32)

    r_copies = []
    for t in range(1, 16):
        partial[t] = total(t).astype(jnp.bfloat16)
        r_copies.append(send(partial.at[t], arrived.at[t], p_send.at[t], p_recv.at[t], plane_peer(t)))
    own_sum[...] = total(0)

    for copy in h_copies:
        copy.wait_recv()
    index = lax.axis_index("blk") * 16 + lax.axis_index("grp")
    places = lax.broadcasted_iota(jnp.int32, (2 * n, n), 0)
    mixing = jnp.zeros((2 * n, n), jnp.float32)
    for slot in range(6):
        mixing += jnp.where(places == neighbours[slot : slot + 1, :], kappa[slot : slot + 1, :], 0.0)
    first = jnp.where(index == 0, 0.0, 1.0)
    last = jnp.where(index == 255, 0.0, 1.0)
    mixing_halo = mixing[n:] * jnp.where(rows < 64, first, last)
    halo_t = halo[...]
    for i in range(2):
        coupled = exact_dot(field[i], mixing[:n]) + exact_dot(halo_t[:, i * n : (i + 1) * n].T, mixing_halo)
        out[1 - i] = coupled if i == 0 else -coupled
    modulus = field[0] * field[0] + field[1] * field[1]
    linear_real = pump[...] - modulus
    linear_imag = detuning[...] - alpha_factor * modulus
    out[0] += linear_real * field[0] - linear_imag * field[1]
    out[1] += linear_real * field[1] + linear_imag * field[0]

    for copy in r_copies:
        copy.wait_recv()
    fresnel = own_sum[...]
    for t in range(1, 16):
        fresnel += arrived[t].astype(jnp.float32)
    fresnel = fresnel * 2.0**-7
    for i in range(2):
        out[i] += fresnel[:, i * n : (i + 1) * n].T
    for copy in pending:
        copy.wait_send()


def local(state, prev_slope, positions, pump, detuning, kappa, neighbours, send_list):
    dma = pltpu.SemaphoreType.DMA
    return pl.pallas_call(
        kernel,
        out_shape=jax.ShapeDtypeStruct(state.shape, jnp.float32),
        in_specs=[pl.BlockSpec(memory_space=pltpu.VMEM)] * 8,
        out_specs=pl.BlockSpec(memory_space=pltpu.VMEM),
        scratch_shapes=[
            pltpu.VMEM((4096, 256), jnp.bfloat16),
            pltpu.VMEM((16, 2, 128), jnp.float32),
            pltpu.VMEM((16, 2, 128), jnp.float32),
            pltpu.VMEM((16, 128, 4096), jnp.bfloat16),
            pltpu.VMEM((16, 128, 256), jnp.bfloat16),
            pltpu.VMEM((16, 128, 256), jnp.bfloat16),
            pltpu.VMEM((128, 256), jnp.float32),
            pltpu.VMEM((128, 256), jnp.float32),
            pltpu.VMEM((128, 256), jnp.float32),
        ]
        + [dma((16,))] * 8
        + [dma((2,))] * 2,
        compiler_params=pltpu.CompilerParams(
            collective_id=0, has_side_effects=True, vmem_limit_bytes=48 * 2**20
        ),
    )(state, prev_slope, positions, pump.reshape(1, -1), detuning.reshape(1, -1), kappa, neighbours, send_list)


def solution(mesh):
    last, flat = P(None, ("blk", "grp")), P(("blk", "grp"))
    whole = P(None, None, ("blk", "grp"))
    return jax.shard_map(
        local,
        mesh=mesh,
        in_specs=(whole, whole, last, flat, flat, last, last, last),
        out_specs=whole,
        check_vma=False,
    )
```

time: 357 us -> 62.6 us (0.18)
  the two profiles are of different devices: /device:TPU:8 before, /device:TPU:1 now
where the time goes in v1:
time: 62.6 us; the launch traced here: 62.4 us
  Pallas kernels  57.8 us (92%)
  local copies, waits for them, and re-layouts  4.54 us (7%)
    pallas_call x1, Pallas kernels, local(): pl.pallas_call(kernel, out_shape=jax.ShapeDtypeStruct(state.shape, jnp.fl...  57.8 us
    unnamed x17, local copies, waits for them, and re-layouts  4.54 us

profile of v1, /device:TPU:1, one launch (start us, length us, event | category | flops | bytes accessed | tf_op | source)
XLA Modules:
  0.0 62.4 jit_solution(7805846414248543370)
XLA Ops:
  0.0 0.0 copy-start.5
  0.0 0.0 copy-start.7
  0.0 0.0 copy-start.4
  0.0 0.0 copy-start.6
  0.0 0.7 %copy-done.5 = s32[2,64]{1,0:T(2,128)S(1)} copy-done((s32[2,64]{1,0:T(2,128)S(1)}, s32[2,64]{1,0:T(2,128)}, u32[]{:S(2)}) %copy-start.5) | copy-done | bytes 536
  0.7 0.0 copy-done.7
  0.7 0.0 copy-done.4
  0.7 0.0 copy-done.6
  0.7 0.0 copy-start
  0.7 0.9 %copy-done = f32[2,128,128]{2,1,0:T(8,128)S(1)} copy-done((f32[2,128,128]{2,1,0:T(8,128)S(1)}, f32[2,128,128]{2,1,0:T(8,128)}, u32[]{:S(2)}) %copy-start) | copy-done | bytes 131096
  1.6 0.0 copy-start.1
  1.6 0.9 %copy-done.1 = f32[2,128,128]{2,1,0:T(8,128)S(1)} copy-done((f32[2,128,128]{2,1,0:T(8,128)S(1)}, f32[2,128,128]{2,1,0:T(8,128)}, u32[]{:S(2)}) %copy-start.1) | copy-done | bytes 131096
  2.5 0.0 copy-start.2
  2.5 0.7 %copy-done.2 = f32[6,128]{1,0:T(8,128)S(1)} copy-done((f32[6,128]{1,0:T(8,128)S(1)}, f32[6,128]{1,0:T(8,128)}, u32[]{:S(2)}) %copy-start.2) | copy-done | bytes 3096
  3.2 0.0 copy-start.3
  3.2 0.7 %copy-done.3 = s32[6,128]{1,0:T(8,128)S(1)} copy-done((s32[6,128]{1,0:T(8,128)S(1)}, s32[6,128]{1,0:T(8,128)}, u32[]{:S(2)}) %copy-start.3) | copy-done | bytes 3096
  3.9 57.8 %shard_map.82 = f32[2,128,128]{2,1,0:T(8,128)S(1)} custom-call(f32[2,128,128]{2,1,0:T(8,128)S(1)} %copy-done, f32[2,128,128]{2,1,0:T(8,128)S(1)} %copy-done.1, f32[2,128]{1,0:T(2,128)S(1)} %copy-done.4, f32[1,128]{1,0:T(1,128)S(1)} %bitcast.2, f32[1,128]{1,0:T(1,128)S(1)} %bitcast.3, f32[6,128]{1,0:T(8,128)S(1)} %copy-done.2, s32[6,128]{1,0:T(8,128)S(1)} %copy-done.3, ...), custom_call_target="tpu_custom_call" | custom-call | tf_op jit(solution)/shard_map/pallas_call | solution.py:188
  61.7 0.7 %copy.10 = f32[2,128,128]{2,1,0:T(8,128)} copy(f32[2,128,128]{2,1,0:T(8,128)S(1)} %shard_map.82) | data formatting | bytes 262144
Async XLA Ops:
  0.0 0.7 %copy-start.5 = (s32[2,64]{1,0:T(2,128)S(1)}, s32[2,64]{1,0:T(2,128)}, u32[]{:S(2)}) copy-start(s32[2,64]{1,0:T(2,128)} %send_list.1) | copy-start | bytes 1540
  0.0 0.7 %copy-start.7 = (f32[128]{0:T(128)S(1)}, f32[128]{0:T(128)}, u32[]{:S(2)}) copy-start(f32[128]{0:T(128)} %param.12) | copy-start | bytes 1540
  0.0 0.7 %copy-start.4 = (f32[2,128]{1,0:T(2,128)S(1)}, f32[2,128]{1,0:T(2,128)}, u32[]{:S(2)}) copy-start(f32[2,128]{1,0:T(2,128)} %positions.1) | copy-start | bytes 3076
  0.0 0.7 %copy-start.6 = (f32[128]{0:T(128)S(1)}, f32[128]{0:T(128)}, u32[]{:S(2)}) copy-start(f32[128]{0:T(128)} %param.11) | copy-start | bytes 1540
  0.7 0.9 %copy-start = (f32[2,128,128]{2,1,0:T(8,128)S(1)}, f32[2,128,128]{2,1,0:T(8,128)}, u32[]{:S(2)}) copy-start(f32[2,128,128]{2,1,0:T(8,128)} %state.1) | copy-start | bytes 393220
  1.6 0.9 %copy-start.1 = (f32[2,128,128]{2,1,0:T(8,128)S(1)}, f32[2,128,128]{2,1,0:T(8,128)}, u32[]{:S(2)}) copy-start(f32[2,128,128]{2,1,0:T(8,128)} %prev_slope.1) | copy-start | bytes 393220
  2.5 0.7 %copy-start.2 = (f32[6,128]{1,0:T(8,128)S(1)}, f32[6,128]{1,0:T(8,128)}, u32[]{:S(2)}) copy-start(f32[6,128]{1,0:T(8,128)} %kappa.1) | copy-start | bytes 9220
  3.2 0.7 %copy-start.3 = (s32[6,128]{1,0:T(8,128)S(1)}, s32[6,128]{1,0:T(8,128)}, u32[]{:S(2)}) copy-start(s32[6,128]{1,0:T(8,128)} %neighbours.1) | copy-start | bytes 9220
